TPU v7x, 256 devices: a whole 4x4x8 slice. The times are simulated.
256 devices in a mesh: fsdp: 64 (over z, y, core), rep: 4 (over x).
Axes of the slice: x: 4, y: 4, z: 8, core: 2. Of those that a mesh axis runs over, the one named last changes fastest.
Arguments:
- grads: float32 [64, 4, 192, 768], P(None, 'rep', 'fsdp'), may hold values from -9 to 9
- params: bfloat16 [64, 4, 192, 768], P(None, 'rep', 'fsdp'), may hold values from -3 to 3
- owner_slot: int32 [64], replicated, may hold values from 0 to 127, as said below
- left_stats: float32 [128, 768, 768], P('fsdp', 'rep'), may hold values from -0.1 to 1, as said below
- right_stats: float32 [128, 768, 768], P('fsdp', 'rep'), may hold values from -0.1 to 1, as said below
- left_root: float32 [128, 768, 768], P('fsdp', 'rep'), may hold values from -0.3 to 2, as said below
- right_root: float32 [128, 768, 768], P('fsdp', 'rep'), may hold values from -0.3 to 2, as said below
Outputs:
- new_params: bfloat16 [64, 4, 192, 768], P(None, 'rep', 'fsdp')
- update: float32 [64, 4, 192, 768], P(None, 'rep', 'fsdp')
- new_left_stats: float32 [128, 768, 768], P('fsdp', 'rep')
- new_right_stats: float32 [128, 768, 768], P('fsdp', 'rep')
Inputs may be any that keep to these rules, and one draw needn't show every extreme that they name: `owner_slot`: the 64 entries are distinct; slot s belongs to the device s // 2 of fsdp; in every draw some device of fsdp holds 2 blocks. `left_stats`: each slot's matrix is symmetric. `right_stats`: each slot's matrix is symmetric. `left_root`: each slot's matrix is symmetric. `right_root`: each slot's matrix is symmetric.
All inputs are finite; a program needn't handle non-finite values.
Results may differ from a plain program's by a relative error of at most 0.001.
Values sent between devices are 32-bit elements; how exact they have to be, the bound alone decides.
A program may use at most 64 MiB of HBM per device.

v0:
```python
import jax
import jax.numpy as jnp
from jax import lax
from jax.sharding import PartitionSpec as P

STAT_DECAY = 0.95
STEP_SIZE = 0.25
EPSILON = 1e-06
HIGHEST_PREC = lax.Precision.HIGHEST


def on_device(grads, params, owner_slot, left_stats, right_stats, left_root, right_root):
    blocks, _, rows_dev, width = grads.shape
    fsdp_count = lax.axis_size("fsdp")
    slots = left_stats.shape[0]
    stripe = left_stats.shape[1]
    slot_count = slots * fsdp_count
    slot_ids = jnp.arange(slot_count, dtype=jnp.int32)
    by_owner = (owner_slot[None, :] == slot_ids[:, None]).astype(jnp.float32)
    by_slot = (
        by_owner.reshape(fsdp_count, slots, blocks).transpose(1, 0, 2).reshape(slot_count, blocks)
    )
    rep_index = lax.axis_index("rep")
    packed = jnp.dot(
        by_slot,
        grads.reshape(blocks, -1),
        precision=HIGHEST_PREC,
        preferred_element_type=jnp.float32,
    )
    packed = packed.reshape(slots, fsdp_count, rows_dev, width)
    arrived = lax.all_to_all(packed, "fsdp", split_axis=1, concat_axis=1, tiled=True)
    own_rows = arrived.reshape(slots, stripe, width)
    whole_grad = lax.all_gather(own_rows, "rep", axis=1, tiled=True)
    own_cols = lax.dynamic_slice_in_dim(whole_grad, rep_index * stripe, stripe, 2)
    left_gram = jnp.einsum(
        "sic,sjc->sij",
        own_rows,
        whole_grad,
        precision=HIGHEST_PREC,
        preferred_element_type=jnp.float32,
    )
    right_gram = jnp.einsum(
        "sci,scj->sij",
        own_cols,
        whole_grad,
        precision=HIGHEST_PREC,
        preferred_element_type=jnp.float32,
    )
    new_left = STAT_DECAY * left_stats + (1.0 - STAT_DECAY) * left_gram
    new_right = STAT_DECAY * right_stats + (1.0 - STAT_DECAY) * right_gram
    right_part = jnp.einsum(
        "sac,sjc->saj",
        whole_grad,
        right_root,
        precision=HIGHEST_PREC,
        preferred_element_type=jnp.float32,
    )
    precond = jnp.einsum(
        "sic,scj->sij",
        left_root,
        lax.all_gather(right_part, "rep", axis=2, tiled=True),
        precision=HIGHEST_PREC,
        preferred_element_type=jnp.float32,
    )
    grad_mean = jnp.mean(whole_grad * whole_grad, axis=(1, 2))
    part_squares = jnp.sum(precond * precond, axis=(1, 2))
    prec_squares = lax.psum(part_squares, "rep")
    graft_scale = jnp.sqrt(grad_mean / (prec_squares / (width * width) + EPSILON))
    grafted = precond * graft_scale[:, None, None]
    returned = lax.all_to_all(
        grafted.reshape(slots, fsdp_count, rows_dev, width),
        "fsdp",
        split_axis=1,
        concat_axis=0,
        tiled=True,
    )
    update = jnp.einsum(
        "sb,sx->bx",
        by_owner,
        returned.reshape(slot_count, -1),
        precision=HIGHEST_PREC,
        preferred_element_type=jnp.float32,
    )
    update = update.reshape(blocks, 1, rows_dev, width)
    new_params = (params.astype(jnp.float32) - STEP_SIZE * update).astype(jnp.bfloat16)
    return (new_params, update, new_left, new_right)


def solution(mesh):
    in_specs = (
        P(None, "rep", "fsdp", None),
        P(None, "rep", "fsdp", None),
        P(),
        P("fsdp", "rep", None),
        P("fsdp", "rep", None),
        P("fsdp", "rep", None),
        P("fsdp", "rep", None),
    )
    out_specs = (
        P(None, "rep", "fsdp", None),
        P(None, "rep", "fsdp", None),
        P("fsdp", "rep", None),
        P("fsdp", "rep", None),
    )
    return jax.shard_map(
        on_device, mesh=mesh, in_specs=in_specs, out_specs=out_specs, check_vma=False
    )
```

profile of v0, /device:TPU:1, one launch (start us, length us, event | category | flops | bytes accessed | tf_op | source)
XLA Modules:
  0.0 243.3 jit_solution(8444823985636973632)
XLA Ops:
  7.2 2.7 %reduce.1 = f32[64,3,768]{2,1,0:T(4,128)S(1)} reduce(f32[64,1,3,768]{3,1,2,0:T(1,128)} %param.7, f32[]{:T(128)} %constant.32), dimensions={1}, to_apply=%param.7.reduce_sub_computation | reduce | bytes 1179652 | tf_op args[0]
  9.9 0.7 fusion.9
  10.6 0.9 copy.37
  11.5 43.6 %all_to_all.20 = f32[2,64,3,768]{3,0,2,1:T(2,128)S(1)} all-to-all(f32[2,64,3,768]{3,0,2,1:T(2,128)S(1)} %copy.37), channel_id=1, replica_groups=mesh['fsdp'=64,'rep'=4] {'fsdp'}, dimensions={1} | all-to-all | bytes 2359296 | tf_op jit(solution)/shard_map/all_to_all | solution.py:31
  55.1 1.1 copy.38
  56.2 52.5 %all-gather.3.cloned.1.call-done = f32[2,768,768]{2,1,0:T(8,128)} async-done(((f32[2,192,768]{2,1,0:T(8,128)}), f32[2,768,768]{2,1,0:T(8,128)}) %all-gather.3.cloned.1.call-update) | async-done | bytes 4718608 | tf_op jit(solution)/shard_map/all_gather | solution.py:33
  108.7 8.3 %fusion.20 = f32[2,768,192]{1,2,0:T(8,128)} fusion(f32[2,768,768]{2,1,0:T(8,128)} %all-gather.3.cloned.1.call-done, f32[2,192,768]{2,1,0:T(8,128)S(1)} %copy-done.1), kind=kOutput, calls=%fused_computation.26 | convolution fusion | flops 2717908992 | bytes 7077888 | tf_op jit(solution)/shard_map/sac,sjc->saj/dot_general | solution.py:51
  117.1 3.0 %multiply_reduce_fusion = f32[2]{0:T(128)S(1)} fusion(f32[2,768,768]{2,1,0:T(8,128)} %all-gather.3.cloned.1.call-done), kind=kLoop, calls=%fused_computation | loop fusion | flops 2359294 | bytes 4718600 | tf_op jit(solution)/shard_map/reduce_sum | solution.py:65
  120.1 52.7 %all-gather.5.cloned.1.call-done = f32[2,768,768]{1,2,0:T(8,128)} async-done(((f32[2,768,192]{1,2,0:T(8,128)}), f32[2,768,768]{1,2,0:T(8,128)}) %all-gather.5.cloned.1.call-update) | async-done | bytes 4718608 | tf_op jit(solution)/shard_map/all_gather | solution.py:61
  172.8 6.9 %multiply_reduce_fusion.1 = (f32[2]{0:T(128)S(1)}, f32[2,768,192]{1,2,0:T(8,128)S(1)}) fusion(f32[2,768,768]{1,2,0:T(8,128)} %all-gather.5.cloned.1.call-done, f32[2,192,768]{2,1,0:T(8,128)S(1)} %copy-done), kind=kOutput, calls=%fused_computation.8 | convolution fusion | flops 2718498816 | bytes 7077896 | tf_op jit(solution)/shard_map/sic,scj->sij/dot_general | solution.py:58
  179.8 6.8 %psum.7 = f32[2]{0:T(128)S(1)} all-reduce(f32[2]{0:T(128)S(1)} %get-tuple-element.20), channel_id=1, replica_groups=mesh['fsdp'=64,'rep'=4] {'rep'}, use_global_device_ids=true, to_apply=%region_2.0 | all-reduce | flops 2 | bytes 16 | tf_op jit(solution)/shard_map/psum | solution.py:67
  186.6 0.2 multiply_bitcast_fusion
  186.8 2.0 copy.39
  188.7 13.0 %all-to-all-start.1 = ((f32[2,64,3,768]{3,0,2,1:T(2,128)}), f32[2,64,3,768]{3,0,2,1:T(2,128)S(1)}, u32[]{:S(2)}, u32[]{:S(2)}) async-start(f32[2,64,3,768]{3,0,2,1:T(2,128)} %bitcast.6), calls=%async_computation.1 | async-start | bytes 2359296 | tf_op jit(solution)/shard_map/all_to_all | solution.py:70
  201.8 8.4 %fusion.5 = f32[2,192,768]{2,1,0:T(8,128)} fusion(f32[2,768,768]{2,1,0:T(8,128)} %all-gather.3.cloned.1.call-done, s32[]{:T(128)S(6)} %select_n.3, f32[2,192,768]{2,1,0:T(8,128)} %param.11), kind=kOutput, calls=%fused_computation.4 | convolution fusion | flops 2718793728 | bytes 8650756 | tf_op jit(solution)/shard_map/sci,scj->sij/dot_general | solution.py:42
  210.2 8.2 %fusion.8 = f32[2,192,768]{2,1,0:T(8,128)} fusion(f32[2,768,768]{2,1,0:T(8,128)} %all-gather.3.cloned.1.call-done, f32[2,192,768]{2,1,0:T(8,128)S(1)} %copy-done.2, f32[2,192,768]{2,0,1:T(2,128)S(1)} %bitcast.38), kind=kOutput, calls=%fused_computation.6 | convolution fusion | flops 2718793728 | bytes 8257536 | tf_op jit(solution)/shard_map/sic,sjc->sij/dot_general | solution.py:35
  218.4 13.9 %all-to-all-done.1 = f32[2,64,3,768]{3,0,2,1:T(2,128)S(1)} async-done(((f32[2,64,3,768]{3,0,2,1:T(2,128)}), f32[2,64,3,768]{3,0,2,1:T(2,128)S(1)}, u32[]{:S(2)}, u32[]{:S(2)}) %all-to-all-start.1) | async-done | bytes 1179680 | tf_op jit(solution)/shard_map/all_to_all | solution.py:70
  232.4 0.4 copy.40
  232.8 0.2 copy.49
  233.0 0.6 fusion.11
  233.6 0.3 reshape.61
  233.9 1.4 copy.44
  235.3 0.3 subtract_convert_fusion
  235.7 0.7 copy.43
  (16 shorter events, 0.2 us)
Async XLA Ops:
  7.2 165.7 %copy-start = (f32[2,192,768]{2,1,0:T(8,128)S(1)}, f32[2,192,768]{2,1,0:T(8,128)}, u32[]{:S(2)}) copy-start(f32[2,192,768]{2,1,0:T(8,128)} %param.12) | copy-start | bytes 3538948
  7.2 2.7 %copy-start.4 = (s32[64]{0:T(128)S(1)}, s32[64]{0:T(128)}, u32[]{:S(2)}) copy-start(s32[64]{0:T(128)} %param.9) | copy-start | bytes 772
  7.2 101.6 %all-gather.3.cloned.1.call-start = ((), (), s32[]{:S(2)}) async-start(), calls=%async_computation.2 | async-start | bytes 5898240 | tf_op jit(solution)/shard_map/all_gather | solution.py:33
  56.2 52.6 %copy-start.1 = (f32[2,192,768]{2,1,0:T(8,128)S(1)}, f32[2,192,768]{2,1,0:T(8,128)}, u32[]{:S(2)}) copy-start(f32[2,192,768]{2,1,0:T(8,128)} %param.13) | copy-start | bytes 3538948
  56.2 116.6 %all-gather.5.cloned.1.call-start = ((), (), s32[]{:S(2)}) async-start(), calls=%async_computation.3 | async-start | bytes 5898240 | tf_op jit(solution)/shard_map/all_gather | solution.py:61
  188.7 43.6 %all-to-all-start.1 = ((f32[2,64,3,768]{3,0,2,1:T(2,128)}), f32[2,64,3,768]{3,0,2,1:T(2,128)S(1)}, u32[]{:S(2)}, u32[]{:S(2)}) async-start(f32[2,64,3,768]{3,0,2,1:T(2,128)} %bitcast.6), calls=%async_computation.1 | async-start | bytes 2359296 | tf_op jit(solution)/shard_map/all_to_all | solution.py:70
  201.8 8.4 %copy-start.2 = (f32[2,192,768]{2,1,0:T(8,128)S(1)}, f32[2,192,768]{2,1,0:T(8,128)}, u32[]{:S(2)}) copy-start(f32[2,192,768]{2,1,0:T(8,128)} %param.10) | copy-start | bytes 3538948
  233.6 1.8 copy-start.3
Sparse Core Ops, SparseCore 0:
  56.3 52.3 all-gather.2
  117.2 55.5 all-gather.4
where the time goes:
time: 244 us; the launch traced here: 243 us
  waiting for transfers between devices  119 us (49%)
  blocking collectives  50.4 us (21%)
  matrix products  33.1 us (14%)
  between operations  14.2 us (6%)
  starting transfers between devices  13.1 us (5%)
  local copies, waits for them, and re-layouts  7.11 us (3%)
  other arithmetic  6.22 us (3%)
    all_gather x1, waiting for transfers between devices, on_device(): lax.all_gather(right_part, 'rep', axis=2, tiled=True)  52.7 us
    all_gather x1, waiting for transfers between devices, on_device(): whole_grad = lax.all_gather(own_rows, 'rep', axis=1, tiled=True)  52.5 us
    all_to_all x1, blocking collectives, on_device(): lax.all_to_all(packed, 'fsdp', split_axis=1, concat_axis=1, tiled=True)  43.6 us
    all_to_all x1, waiting for transfers between devices, on_device(): lax.all_to_all(grafted.reshape(slots, fsdp_count, rows_dev, width), 'fsdp...  13.9 us
    all_to_all x1, starting transfers between devices, on_device(): lax.all_to_all(grafted.reshape(slots, fsdp_count, rows_dev, width), 'fsdp...  13 us
    dot_general x1, matrix products, on_device(): jnp.einsum('sci,scj->sij', own_cols, whole_grad, precision=HIGHEST_PREC,...  8.43 us
    dot_general x1, matrix products, on_device(): jnp.einsum('sac,sjc->saj', whole_grad, right_root, precision=HIGHEST_PREC...  8.3 us
    dot_general x1, matrix products, on_device(): jnp.einsum('sic,sjc->sij', own_rows, whole_grad, precision=HIGHEST_PREC,...  8.2 us
  transfers between devices with their start and end apart: 3, of which 3 were waited for; matrix products, arithmetic and copies ran while one was open for 8% of the time, Pallas kernels for 0%

commit v1 on v0

v1 whole, which is shorter than its diff:
```python
import functools

import jax
import jax.numpy as jnp
from jax import lax
from jax.experimental import pallas as pl
from jax.experimental.pallas import tpu as pltpu
from jax.sharding import PartitionSpec as P

STAT_DECAY = 0.95
STEP_SIZE = 0.25
EPSILON = 1e-06
LANES = 128
F32 = jnp.float32
BF16 = jnp.bfloat16
NN = (((1,), (0,)), ((), ()))
NT = (((1,), (1,)), ((), ()))


def split(value):
    high = value.astype(BF16)
    return high, (value - high.astype(F32)).astype(BF16)


def dot3(left, right, dims):
    dot = functools.partial(lax.dot_general, dimension_numbers=dims, preferred_element_type=F32)
    return dot(left[0], right[0]) + (dot(left[0], right[1]) + dot(left[1], right[0]))


def kernel(
    nf, nx, rows, groups, blocks,
    slot_block, owner, grads, params, left_root, right_root, left_stats, right_stats,
    update, new_params, new_left, new_right,
    grads_v, send, gath, back, ret, upd_t, left_v, lstat_v, rstat_v,
    root_f, root_h, root_l, gh, gl, gt, lh, ll, lgh, lgl, prec, sq,
    in_sem, out_sem, a_send, a_recv, r_send, r_recv, x_send, x_recv, f_send, f_recv,
    s_send, s_recv, u_send, u_recv,
):
    slots, stripe, width = left_v.shape
    panels = width // LANES
    half = width // 2
    packet = rows * panels
    size = nf // groups
    chunk = size * rows
    me = lax.axis_index("fsdp")
    x = lax.axis_index("rep")
    mz, mg = me // size, me % size
    right_x, left_x, far_x = (x + 1) % nx, (x + nx - 1) % nx, (x + 2) % nx
    h, pos = x // 2, x % 2
    mate = h * 2 + 1 - pos
    other = jnp.where(pos == 0, left_x, right_x)

    def at_x(target):
        return {"fsdp": me, "rep": target}

    def at_f(target):
        return {"fsdp": target, "rep": x}

    def remote(src, dst, send_sem, recv_sem, device):
        return pltpu.make_async_remote_copy(
            src_ref=src, dst_ref=dst, send_sem=send_sem, recv_sem=recv_sem,
            device_id=device, device_id_type=pl.DeviceIdType.MESH,
        )

    def await_bytes(ref, sem):
        pltpu.make_async_copy(ref, ref, sem).wait()

    order = [0]
    for step in range(groups // 2, 0, -1):
        order.append(step)
        if step != groups - step:
            order.append(groups - step)

    load_grads = pltpu.make_async_copy(grads, grads_v.at[pl.ds(0, blocks * packet)], in_sem.at[0])
    load_grads.start()
    load_left = pltpu.make_async_copy(left_root, left_v, in_sem.at[1])
    load_left.start()
    loads_r = []
    for t in range(slots):
        for kind in range(2):
            col = h if kind == 0 else 1 - h
            cols = pl.ds(pl.multiple_of(col * half, LANES), half)
            src = right_root.at[t, :, cols]
            load = pltpu.make_async_copy(
                src, root_f.at[t, kind, pl.ds(pl.multiple_of(pos * stripe, 8), stripe)], in_sem.at[2 + 2 * t + kind]
            )
            load.start()
            loads_r.append(load)
    load_ls = pltpu.make_async_copy(left_stats, lstat_v, in_sem.at[6])
    load_ls.start()
    load_rs = pltpu.make_async_copy(right_stats, rstat_v, in_sem.at[7])
    load_rs.start()

    barrier = pltpu.get_barrier_semaphore()

    def greet(k, carry):
        pl.semaphore_signal(barrier, inc=1, device_id=at_f((me + k) % nf), device_id_type=pl.DeviceIdType.MESH)
        return carry

    lax.fori_loop(1, nf, greet, 0)
    for d in range(1, nx):
        pl.semaphore_signal(barrier, inc=1, device_id=at_x((x + d) % nx), device_id_type=pl.DeviceIdType.MESH)
    pl.semaphore_wait(barrier, nf - 1 + nx - 1)

    root_sends = []
    root_fwds = []
    for t in range(slots):
        for kind in range(2):
            loads_r[2 * t + kind].wait()
        my_rows = pl.ds(pl.multiple_of(pos * stripe, 8), stripe)
        mate_rows = pl.ds(pl.multiple_of((1 - pos) * stripe, 8), stripe)
        group = [
            remote(root_f.at[t, 0, my_rows], root_f.at[t, 2, my_rows], r_send.at[t, 2], r_recv.at[t, 2], at_x(other)),
            remote(root_f.at[t, 0, my_rows], root_f.at[t, 0, my_rows], r_send.at[t, 0], r_recv.at[t, 0], at_x(mate)),
            remote(root_f.at[t, 1, my_rows], root_f.at[t, 1, my_rows], r_send.at[t, 1], r_recv.at[t, 1], at_x(mate)),
        ]
        for copy in group:
            copy.start()
        root_sends += group
        root_fwds.append(
            remote(root_f.at[t, 0, mate_rows], root_f.at[t, 2, mate_rows], r_send.at[t, 3], r_recv.at[t, 3], at_x(other))
        )

    load_grads.wait()
    flat_grads = grads_v.reshape((blocks + 1) * packet, LANES)
    flat_grads[pl.ds(blocks * packet, packet), :] = jnp.zeros((packet, LANES), F32)
    flat_send = send.reshape(slots * nf * packet, LANES)

    def pack(t, dest):
        block = slot_block[slots * dest + t]
        for j in range(rows):
            value = flat_grads[pl.ds(block * packet + panels * j, panels), :]
            flat_send[pl.ds((t * nf + dest) * packet + j, panels, stride=rows), :] = value

    for t in range(slots):
        mine = gath.at[t, x, :, pl.ds(me * rows, rows)]
        pack(t, me)
        pltpu.make_async_copy(send.at[t, me], mine, a_recv.at[t, mz]).start()
        for offset in order:
            dz = (mz + offset) % groups

            def post(k, carry, t=t, dz=dz, mine=mine):
                dest = dz * size + (mg + k) % size
                pack(t, dest)
                remote(send.at[t, dest], mine, a_send.at[t], a_recv.at[t, mz], at_f(dest)).start()
                return carry

            lax.fori_loop(1 if offset == 0 else 0, size, post, 0)

    load_left.wait()
    for t in range(slots):
        lh[t], ll[t] = split(left_v[t])

    def rows_of(k):
        source = (mz + groups - order[k]) % groups
        return source, pl.ds(source * chunk, chunk)

    def direct(t, k, side):
        source, part = rows_of(k)
        ref = gath.at[t, x, :, part]
        return remote(ref, ref, x_send.at[t, side, k], x_recv.at[t, side, k], at_x(right_x if side == 0 else left_x))

    def arrival(t, k, side):
        source, part = rows_of(k)
        ref = gath.at[t, left_x if side == 0 else right_x, :, part]
        return remote(ref, ref, x_send.at[t, side, k], x_recv.at[t, side, k], at_x(right_x if side == 0 else left_x))

    def forward(t, k):
        source, part = rows_of(k)
        side = k % 2
        ref = gath.at[t, left_x if side == 0 else right_x, :, part]
        return remote(ref, ref, f_send.at[t, k], f_recv.at[t, k], at_x(right_x if side == 0 else left_x))

    def far_arrival(t, k):
        source, part = rows_of(k)
        ref = gath.at[t, far_x, :, part]
        return remote(ref, ref, f_send.at[t, k], f_recv.at[t, k], at_x(right_x))

    def spread(t):
        for k in range(groups):
            source, part = rows_of(k)
            await_bytes(gath.at[t, x, :, part], a_recv.at[t, source])
            direct(t, k, 0).start()
            direct(t, k, 1).start()

    def relay(t):
        for k in range(groups):
            side = k % 2
            arrival(t, k, side).wait_recv()
            forward(t, k).start()

    g4 = gath.reshape(slots, nx, panels, stripe, LANES)
    ret4 = ret.reshape(slots, panels, stripe, LANES)

    def take(t, i):
        total = jnp.zeros((1, LANES), F32)
        part = pl.ds(pl.multiple_of(i * stripe, 16), stripe)
        for c in range(panels):
            value = g4[t, i, c]
            total = total + jnp.sum(value * value, axis=0, keepdims=True)
            high, low = split(value)
            gh[t, part, c * LANES : (c + 1) * LANES] = high
            gl[t, part, c * LANES : (c + 1) * LANES] = low
        return total

    def take_root(t):
        for kind in range(3):
            root_h[t, kind], root_l[t, kind] = split(root_f[t, kind])

    def precondition(t):
        for c in range(2):
            cols = slice(c * half, (c + 1) * half)
            mixed = dot3((lh[t], ll[t]), (gh[t, :, cols], gl[t, :, cols]), NN)
            lgh[c], lgl[c] = split(mixed)
        near = (lgh[h], lgl[h])
        away = (lgh[1 - h], lgl[1 - h])
        root = [(root_h[t, kind], root_l[t, kind]) for kind in range(3)]
        prec_near = dot3(near, root[0], NN) + dot3(away, root[1], NT)
        prec_away = dot3(near, root[1], NN) + dot3(away, root[2], NN)
        squares = jnp.sum(prec_near * prec_near + prec_away * prec_away, axis=0, keepdims=True)
        per = half // LANES
        for c in range(per):
            cols = slice(c * LANES, (c + 1) * LANES)
            prec[h * per + c] = prec_near[:, cols]
            prec[(1 - h) * per + c] = prec_away[:, cols]
        sq[t, x] = jnp.broadcast_to(jnp.sum(squares, axis=1, keepdims=True), sq.shape[2:])
        for d in range(1, nx):
            remote(sq.at[t, x], sq.at[t, x], s_send.at[t, d - 1], s_recv.at[t, d - 1], at_x((x + d) % nx)).start()

    def square_wait(t):
        for d in range(1, nx):
            source = (x + nx - d) % nx
            remote(sq.at[t, source], sq.at[t, source], s_send.at[t, d - 1], s_recv.at[t, d - 1], at_x((x + d) % nx)).wait_recv()

    def give_back(t, grad_squares):
        prec_mean = (((sq[t, 0] + sq[t, 1]) + sq[t, 2]) + sq[t, 3]) / (width * width)
        grad_mean = jnp.sum(grad_squares, axis=1, keepdims=True) / (width * width)
        scale = jnp.sqrt(grad_mean / (prec_mean[0:1, :] + EPSILON))
        for c in range(panels):
            ret4[t, c] = prec[c] * scale
        own = ret.at[t, :, pl.ds(me * rows, rows)]
        pltpu.make_async_copy(own, back.at[t, me], u_recv.at[t]).start()
        for offset in order:
            dz = (mz + offset) % groups

            def post(k, carry, dz=dz):
                dest = dz * size + (mg + k) % size
                remote(
                    ret.at[t, :, pl.ds(dest * rows, rows)], back.at[t, me], u_send.at[t], u_recv.at[t], at_f(dest)
                ).start()
                return carry

            lax.fori_loop(1 if offset == 0 else 0, size, post, 0)

    def left_gram(t):
        mine = pl.ds(pl.multiple_of(x * stripe, 16), stripe)
        ours = (gh[t, mine], gl[t, mine])
        for n in range(3):
            part = slice(n * 256, (n + 1) * 256)
            gram = dot3(ours, (gh[t, part], gl[t, part]), NT)
            lstat_v[t, :, part] = STAT_DECAY * lstat_v[t, :, part] + (1.0 - STAT_DECAY) * gram
        pltpu.make_async_copy(lstat_v.at[t], new_left.at[t], out_sem.at[t]).start()

    def right_gram(t):
        first = (3 * x) // 2
        for i in range(nx):
            pair = jnp.concatenate([g4[t, i, first], g4[t, i, first + 1]], axis=1)
            gt[:, i * stripe : (i + 1) * stripe] = pair.T
        ours = split(gt[pl.ds(pl.multiple_of(pos * (LANES // 2), 8), stripe), :])
        for n in range(3):
            part = slice(n * 256, (n + 1) * 256)
            gram = dot3(ours, (gh[t, :, part], gl[t, :, part]), NN)
            rstat_v[t, :, part] = STAT_DECAY * rstat_v[t, :, part] + (1.0 - STAT_DECAY) * gram
        pltpu.make_async_copy(rstat_v.at[t], new_right.at[t], out_sem.at[2 + t]).start()

    def root_relay(t):
        remote(
            root_f.at[t, 0, mate_rows], root_f.at[t, 0, mate_rows], r_send.at[t, 0], r_recv.at[t, 0], at_x(mate)
        ).wait_recv()
        root_fwds[t].start()

    def root_finish(t):
        remote(
            root_f.at[t, 1, mate_rows], root_f.at[t, 1, mate_rows], r_send.at[t, 1], r_recv.at[t, 1], at_x(mate)
        ).wait_recv()
        remote(
            root_f.at[t, 2, mate_rows], root_f.at[t, 2, mate_rows], r_send.at[t, 2], r_recv.at[t, 2], at_x(other)
        ).wait_recv()
        remote(
            root_f.at[t, 2, my_rows], root_f.at[t, 2, my_rows], r_send.at[t, 3], r_recv.at[t, 3], at_x(other)
        ).wait_recv()

    def gather_rest(t, sides):
        for k in range(groups):
            if k % 2 != sides:
                continue
            arrival(t, k, 1 - sides).wait_recv()

    totals = [None] * slots
    root_relay(0)
    spread(0)
    root_relay(1)
    relay(0)
    spread(1)
    root_finish(0)
    take_root(0)
    for t in range(slots):
        totals[t] = take(t, x)
        gather_rest(t, 0)
        gather_rest(t, 1)
        totals[t] = totals[t] + take(t, left_x) + take(t, right_x)
        for k in range(groups):
            far_arrival(t, k).wait_recv()
        totals[t] = totals[t] + take(t, far_x)
        precondition(t)
        if t == 0:
            load_ls.wait()
            load_rs.wait()
            relay(1)
            square_wait(0)
            give_back(0, totals[0])
            left_gram(0)
            root_finish(1)
            take_root(1)
        else:
            square_wait(1)
            give_back(1, totals[1])
            right_gram(0)
            left_gram(1)
            right_gram(1)

    flat_back = back.reshape(slots * nf * packet, LANES)
    for t in range(slots):
        await_bytes(back.at[t], u_recv.at[t])

    def place(b, carry):
        slot = owner[b]
        start = ((slot % slots) * nf + slot // slots) * packet
        for c in range(panels):
            value = flat_back[pl.ds(start + rows * c, rows), :]
            update[pl.ds(b * packet + c, rows, stride=panels), :] = value
            upd_t[pl.ds(c * blocks + b, rows, stride=panels * blocks), :] = value
        return carry

    lax.fori_loop(0, blocks, place, 0)
    for j in range(rows):
        for c in range(panels):
            cols = slice(c * LANES, (c + 1) * LANES)
            step = STEP_SIZE * upd_t[(j * panels + c) * blocks : (j * panels + c + 1) * blocks, :]
            new_params[j, :, cols] = (params[j, :, cols].astype(F32) - step).astype(BF16)

    for t in range(slots):
        pltpu.make_async_copy(lstat_v.at[t], new_left.at[t], out_sem.at[t]).wait()
        pltpu.make_async_copy(rstat_v.at[t], new_right.at[t], out_sem.at[2 + t]).wait()
        await_bytes(send.at[t, pl.ds(0, nf - 1)], a_send.at[t])
        await_bytes(back.at[t, pl.ds(0, nf - 1)], u_send.at[t])
        for k in range(groups):
            direct(t, k, 0).wait_send()
            direct(t, k, 1).wait_send()
            forward(t, k).wait_send()
        for d in range(1, nx):
            remote(sq.at[t, x], sq.at[t, x], s_send.at[t, d - 1], s_recv.at[t, d - 1], at_x((x + d) % nx)).wait_send()
    for copy in root_sends:
        copy.wait_send()
    for copy in root_fwds:
        copy.wait_send()


def on_device(grads, params, owner_slot, left_stats, right_stats, left_root, right_root):
    blocks, _, rows, width = grads.shape
    nf = lax.axis_size("fsdp")
    nx = lax.axis_size("rep")
    slots, stripe, _ = left_stats.shape
    panels = width // LANES
    half = width // 2
    packet = rows * panels
    groups = 8 if nf >= 64 else 2
    slot_ids = jnp.arange(slots * nf, dtype=jnp.int32)
    block_ids = jnp.arange(blocks, dtype=jnp.int32)
    slot_block = jnp.min(
        jnp.where(owner_slot[None, :] == slot_ids[:, None], block_ids[None, :], blocks), axis=1
    )
    flat = grads.reshape(blocks * packet, 1, LANES)
    params_t = params.reshape(blocks, rows, width).transpose(1, 0, 2)
    hbm = pl.BlockSpec(memory_space=pl.ANY)
    vmem = pl.BlockSpec(memory_space=pltpu.VMEM)
    smem = pl.BlockSpec(memory_space=pltpu.SMEM)
    dma = pltpu.SemaphoreType.DMA
    update, new_params, new_left, new_right = pl.pallas_call(
        functools.partial(kernel, nf, nx, rows, groups, blocks),
        out_shape=(
            jax.ShapeDtypeStruct((blocks * packet, LANES), F32),
            jax.ShapeDtypeStruct((rows, blocks, width), BF16),
            jax.ShapeDtypeStruct(left_stats.shape, F32),
            jax.ShapeDtypeStruct(right_stats.shape, F32),
        ),
        in_specs=[smem, smem, hbm, vmem, hbm, hbm, hbm, hbm],
        out_specs=(vmem, vmem, hbm, hbm),
        scratch_shapes=[
            pltpu.VMEM(((blocks + 1) * packet, 1, LANES), F32),
            pltpu.VMEM((slots, nf, panels, rows, 1, LANES), F32),
            pltpu.VMEM((slots, nx, panels, stripe, 1, LANES), F32),
            pltpu.VMEM((slots, nf, panels, rows, 1, LANES), F32),
            pltpu.VMEM((slots, panels, stripe, 1, LANES), F32),
            pltpu.VMEM((blocks * packet, LANES), F32),
            pltpu.VMEM((slots, stripe, width), F32),
            pltpu.VMEM((slots, stripe, width), F32),
            pltpu.VMEM((slots, stripe, width), F32),
            pltpu.VMEM((slots, 3, half, half), F32),
            pltpu.VMEM((slots, 3, half, half), BF16),
            pltpu.VMEM((slots, 3, half, half), BF16),
            pltpu.VMEM((slots, width, width), BF16),
            pltpu.VMEM((slots, width, width), BF16),
            pltpu.VMEM((2 * LANES, width), F32),
            pltpu.VMEM((slots, stripe, width), BF16),
            pltpu.VMEM((slots, stripe, width), BF16),
            pltpu.VMEM((2, stripe, half), BF16),
            pltpu.VMEM((2, stripe, half), BF16),
            pltpu.VMEM((panels, stripe, LANES), F32),
            pltpu.VMEM((slots, nx, 8, LANES), F32),
            dma((8,)),
            dma((4,)),
            dma((slots,)),
            dma((slots, groups)),
            dma((slots, 4)),
            dma((slots, 4)),
            dma((slots, 2, groups)),
            dma((slots, 2, groups)),
            dma((slots, groups)),
            dma((slots, groups)),
            dma((slots, nx - 1)),
            dma((slots, nx - 1)),
            dma((slots,)),
            dma((slots,)),
        ],
        compiler_params=pltpu.CompilerParams(
            collective_id=0, has_side_effects=True, vmem_limit_bytes=56 * 1024 * 1024
        ),
    )(slot_block, owner_slot, flat, params_t, left_root, right_root, left_stats, right_stats)
    update = update.reshape(blocks, 1, rows, width)
    new_params = new_params.transpose(1, 0, 2).reshape(blocks, 1, rows, width)
    return (new_params, update, new_left, new_right)


def solution(mesh):
    in_specs = (
        P(None, "rep", "fsdp", None),
        P(None, "rep", "fsdp", None),
        P(),
        P("fsdp", "rep", None),
        P("fsdp", "rep", None),
        P("fsdp", "rep", None),
        P("fsdp", "rep", None),
    )
    out_specs = (
        P(None, "rep", "fsdp", None),
        P(None, "rep", "fsdp", None),
        P("fsdp", "rep", None),
        P("fsdp", "rep", None),
    )
    return jax.shard_map(
        on_device, mesh=mesh, in_specs=in_specs, out_specs=out_specs, check_vma=False
    )
```

time: 244 us -> 113 us (0.46)
  waiting for transfers between devices: 119 us -> 0 us
  Pallas kernels: 0 us -> 104 us
  blocking collectives: 50.4 us -> 0 us
  matrix products: 33.1 us -> 0 us
  between operations: 14.2 us -> 0.65 us
  starting transfers between devices: 13.1 us -> 0 us
  other arithmetic: 6.22 us -> 1.26 us
    all_gather x2 -> x0, waiting for transfers between devices: 105 us -> none  [the longest x1 52.7 us: on_device(): lax.all_gather(right_part, 'rep', axis=2, tiled=True)]
    pallas_call x0 -> x1, Pallas kernels: none -> 104 us  [on_device(): pl.pallas_call(functools.partial(kernel, nf, nx, rows, groups, blocks), o...]
    all_to_all x1 -> x0, blocking collectives: 43.6 us -> none  [on_device(): lax.all_to_all(packed, 'fsdp', split_axis=1, concat_axis=1, tiled=True)]
    dot_general x6 -> x0, matrix products: 33.1 us -> none  [the longest x1 8.43 us: on_device(): jnp.einsum('sci,scj->sij', own_cols, whole_grad, precision=HIGHEST_PREC,...]
    all_to_all x1 -> x0, waiting for transfers between devices: 13.9 us -> none  [on_device(): lax.all_to_all(grafted.reshape(slots, fsdp_count, rows_dev, width), 'fsdp...]
    all_to_all x1 -> x0, starting transfers between devices: 13 us -> none  [on_device(): lax.all_to_all(grafted.reshape(slots, fsdp_count, rows_dev, width), 'fsdp...]
    psum x1 -> x0, blocking collectives: 6.84 us -> none  [on_device(): prec_squares = lax.psum(part_squares, 'rep')]
    unnamed x13 -> x8, local copies, waits for them, and re-layouts: 2.41 us -> 6.78 us
  transfers between devices with their start and end apart: 3 -> 0, of which waited for: 3 -> 0; matrix products, arithmetic and copies ran while one was open for 8% -> 0% of each run, Pallas kernels for 0% -> 0%
where the time goes in v1:
time: 113 us
  Pallas kernels  104 us (92%)
  local copies, waits for them, and re-layouts  6.78 us (6%)
  other arithmetic  1.26 us (1%)
    pallas_call x1, Pallas kernels, on_device(): pl.pallas_call(functools.partial(kernel, nf, nx, rows, groups, blocks), o...  104 us
    unnamed x8, local copies, waits for them, and re-layouts  6.78 us

profile of v1, /device:TPU:1, one launch (start us, length us, event | category | flops | bytes accessed | tf_op | source)
XLA Modules:
  0.0 113.2 jit_solution(4517789754914097744)
XLA Ops:
  0.6 1.3 %select_reduce_fusion.slot_block = s32[128]{0:T(128)} fusion(s32[64]{0:T(128)} %owner.1), kind=kLoop, calls=%fused_computation | loop fusion | flops 24448 | bytes 768 | tf_op jit(solution)/shard_map/reduce_min | solution.py:380
  1.9 104.5 %shard_map.102 = (f32[1152,128]{1,0:T(8,128)}, bf16[3,64,768]{2,1,0:T(8,128)(2,1)}, f32[2,192,768]{2,1,0:T(8,128)}, f32[2,192,768]{2,1,0:T(8,128)}) custom-call(s32[128]{0:T(128)} %select_reduce_fusion.slot_block, s32[64]{0:T(128)} %owner.1, f32[1152,1,128]{2,1,0:T(1,128)} %bitcast.8, bf16[3,64,768]{2,1,0:T(8,128)(2,1)} %bitcast.10, ...), custom_call_target="tpu_custom_call" | custom-call | tf_op jit(solution)/shard_map/pallas_call | solution.py:389
  106.4 0.0 copy-start.1
  106.4 1.8 %copy.18 = bf16[64,1,3,768]{3,0,2,1:T(8,128)(2,1)} copy(bf16[64,1,3,768]{3,0,2,1:T(8,128)(2,1)} %bitcast.11) | data formatting | bytes 589824
  108.2 2.3 %copy.19 = f32[64,1,3,768]{3,1,2,0:T(1,128)} copy(f32[64,1,3,768]{3,1,2,0:T(1,128)} %bitcast.9) | data formatting | bytes 1179648
  110.5 0.0 copy-done.1
  110.5 0.0 copy-start
  110.5 1.0 copy.20
  111.5 0.7 copy-done
  112.2 1.0 copy.21
Async XLA Ops:
  106.4 4.1 %copy-start.1 = (f32[2,192,768]{2,1,0:T(8,128)S(1)}, f32[2,192,768]{2,1,0:T(8,128)}, u32[]{:S(2)}) copy-start(f32[2,192,768]{2,1,0:T(8,128)} %get-tuple-element.30) | copy-start | bytes 3538948
  110.5 1.7 %copy-start = (f32[2,192,768]{2,1,0:T(8,128)S(1)}, f32[2,192,768]{2,1,0:T(8,128)}, u32[]{:S(2)}) copy-start(f32[2,192,768]{2,1,0:T(8,128)} %get-tuple-element.31) | copy-start | bytes 3538948
